TPU v7x, 32 devices: a whole 2x2x4 slice. The times are simulated.
32 devices in a mesh: row: 8 (over z, core), col: 4 (over y, x).
Axes of the slice: x: 2, y: 2, z: 4, core: 2. Of those that a mesh axis runs over, the one named last changes fastest.
Arguments:
- front_entries: float32 [16384, 16384], P('row', 'col'), may hold values from 0 to 3, as said below
- tile_group: int32 [32], replicated, may hold values from 0 to 3
- child_factor: bfloat16 [16384, 256], P('row', 'col'), may hold values from -0.375 to 0.375
- row_map: int32 [128], replicated, may hold values from 0 to 127, as said below
Outputs:
- factor_panels: bfloat16 [16384, 512], P('row', 'col')
- schur_block: float32 [16384, 16384], P('row', 'col')
Inputs may be any that keep to these rules, and one draw needn't show every extreme that they name: `front_entries`: Symmetric; assembled is positive definite. `row_map`: A permutation of the parent tiles. The tile in row block r (blocks of 2048 rows) goes to a parent tile in row block r or in the row block whose index differs from r in the highest bit.
All inputs are finite; a program needn't handle non-finite values.
Results may differ from a plain program's by a relative error of at most 0.0026.
Values may be sent and summed in bfloat16 or wider, within the bound.
No kernel may reach another device: no remote copies, remote signals or barrier semaphores. Data moves between devices by JAX's collectives and lax.ppermute only.
A program may use at most 192 MiB of HBM per device.

v0:
```python
import functools

import jax
import jax.numpy as jnp
from jax import lax
from jax.experimental import pallas as pl
from jax.experimental.pallas import tpu as pltpu
from jax.sharding import PartitionSpec as P

PW = 256
NP = 2
TS = 128
MT = 512
NPIV = NP * PW
BLK = 32
F32 = jnp.float32
BF16 = jnp.bfloat16
VMEM_BYTES = 60 * 1024 * 1024

NN = (((1,), (0,)), ((), ()))
NT = (((1,), (1,)), ((), ()))
TN = (((0,), (0,)), ((), ()))


def dot(left, right, dims=NN, precision=None):
    return lax.dot_general(left, right, dims, precision=precision, preferred_element_type=F32)


def exact(left, right, dims=NN):
    return dot(left, right, dims, lax.Precision.HIGHEST)


def split(value):
    high = value.astype(BF16)
    return high, (value - high.astype(F32)).astype(BF16)


def swapped(value, axis, mask):
    if mask == 0:
        return value
    return lax.ppermute(value, axis, [(i, i ^ mask) for i in range(lax.axis_size(axis))])


def whole_spec():
    return pl.BlockSpec(memory_space=pltpu.VMEM)


def any_spec():
    return pl.BlockSpec(memory_space=pl.ANY)


def smem_spec():
    return pl.BlockSpec(memory_space=pltpu.SMEM)


def factor_diagonal(block):
    groups = BLK // 8
    lane = lax.broadcasted_iota(jnp.int32, (BLK, 128), 1)
    row = lax.broadcasted_iota(jnp.int32, (BLK, 128), 0)
    row8 = lax.broadcasted_iota(jnp.int32, (8, 128), 0)
    start = jnp.where(lane < BLK, block, jnp.where(lane == row + BLK, 1.0, 0.0))
    work = [start[8 * g : 8 * g + 8] for g in range(groups)]
    cols = []
    for k in range(BLK):
        base = 8 * (k // 8)
        cols.append(jnp.broadcast_to(block[base:, k : k + 1], (BLK - base, 128)))
    scale = [jnp.ones((8, 128), F32) for _ in range(groups)]

    def inverse_root(value):
        root = lax.rsqrt(value)
        return root * (1.5 - 0.5 * value * root * root)

    for j in range(0, BLK, 2):
        g0 = j // 8
        base = 8 * g0
        one, two = cols[j], cols[j + 1]
        first, cross, last = one[j - base : j - base + 1], one[j - base + 1 : j - base + 2], two[j - base + 1 : j - base + 2]
        volume = first * last - cross * cross
        root = inverse_root(volume)
        inverse = root * root
        below = row[base:] > j + 1
        lead_one = jnp.where(below, last * one - cross * two, 0.0) * inverse
        lead_two = jnp.where(below, first * two - cross * one, 0.0) * inverse
        row_one, row_two = work[g0][j - base : j - base + 1], work[g0][j - base + 1 : j - base + 2]
        for k in range(j + 2, BLK):
            skip = 8 * (k // 8 - g0)
            cols[k] = cols[k] - (
                lead_one[skip:] * one[k - base : k - base + 1] + lead_two[skip:] * two[k - base : k - base + 1]
            )
        for g in range(g0, groups):
            part = slice(8 * (g - g0), 8 * (g - g0) + 8)
            work[g] = work[g] - (lead_one[part] * row_one + lead_two[part] * row_two)
        first_root = inverse_root(first)
        ratio = cross * (first_root * first_root)
        work[g0] = work[g0] - jnp.where(row8 == j - base + 1, ratio, 0.0) * row_one
        scale[g0] = jnp.where(row8 == j - base, first_root, scale[g0])
        scale[g0] = jnp.where(row8 == j - base + 1, first * first_root * root, scale[g0])
    return jnp.concatenate([work[g] * scale[g] for g in range(groups)], axis=0)


def factor_panel(work, upper_out, start, stop):
    per_tile = 128 // BLK
    row = lax.broadcasted_iota(jnp.int32, (BLK, PW), 0)
    lane = lax.broadcasted_iota(jnp.int32, (BLK, PW), 1)
    all_lane = lax.broadcasted_iota(jnp.int32, (PW, PW), 1)

    def step(b, carry):
        low = pl.multiple_of(b * BLK, BLK)
        tile = pl.multiple_of((b // per_tile) * 128, 128)
        shift = (b % per_tile) * BLK
        block = pltpu.roll(work[pl.ds(low, BLK), pl.ds(tile, 128)], (128 - shift) % 128, 1)
        done = factor_diagonal(block)
        inverse = pltpu.roll(done, 128 - BLK, 1)[:, :BLK]
        inside = (lane >= low) & (lane < low + BLK)
        lines = jnp.where(inside, jnp.where(lane == row + low, 1.0, 0.0), work[pl.ds(low, BLK), :])
        upper = exact(inverse, lines)
        placed = pltpu.roll(done, shift, 1)
        corner = jnp.concatenate([placed] * (PW // 128), axis=1)
        upper_out[pl.ds(low, BLK), :] = jnp.where(inside, corner, upper)
        lead = jnp.where(lane >= low + BLK, upper, 0.0)
        kept = jnp.where((all_lane >= low) & (all_lane < low + BLK), 0.0, work[...])
        work[...] = kept - exact(lead, upper, TN)
        work[pl.ds(low, BLK), :] = upper
        return carry

    lax.fori_loop(start, stop, step, 0)


def diagonals(value):
    row = lax.broadcasted_iota(jnp.int32, (PW, PW), 0)
    col = lax.broadcasted_iota(jnp.int32, (PW, PW), 1)
    kept = jnp.where(row == col, value, 0.0)
    return jnp.sum(kept, axis=1, keepdims=True), jnp.sum(kept, axis=0, keepdims=True)


def start_panel(work, diag_col, diag_row, value):
    by_row, by_col = diagonals(value)
    diag_col[...] = jnp.broadcast_to(by_row, (PW, 128))
    diag_row[...] = jnp.broadcast_to(by_col, (8, PW))
    work[...] = value / jnp.sqrt(by_row) / jnp.sqrt(by_col)


def pivot_values(table, stride, share, along_rows):
    shape = (NPIV, 1) if along_rows else (1, NPIV)
    block = lax.broadcasted_iota(jnp.int32, shape, 0 if along_rows else 1) % PW // share
    values = jnp.zeros(shape, F32)
    for r in range(PW // share):
        values = jnp.where(block == r, table[r * stride], values)
    return values


def tile_values(table, start, count):
    return jnp.concatenate([jnp.full((1, TS), table[start + i], F32) for i in range(count)], axis=1)


def finish_panel(work, upper, diag_col, diag_row, lower, inv_hi, inv_lo, inv_t_hi, inv_t_lo):
    row = lax.broadcasted_iota(jnp.int32, (PW, PW), 0)
    col = lax.broadcasted_iota(jnp.int32, (PW, PW), 1)
    lower[:PW, :] = jnp.where(col <= row, upper[...].T, 0.0) * jnp.sqrt(diag_col[:, :1])
    inverse = jnp.where(col <= row, work[...], 0.0) / jnp.sqrt(diag_row[:1, :])
    inv_hi[...], inv_lo[...] = split(inverse)
    inv_t_hi[...], inv_t_lo[...] = split(inverse.T)
    return inverse


def open_kernel(sizes, place, group_of, kid_of, near, far,
                work, upper, diag_col, diag_row, low_rows, piv_t, piv, pile, wide):
    cols, fan, share, held, tiles = sizes
    my_row, my_col = place[0], place[1]
    my_q, my_a = my_row % fan, my_row // fan
    col_share = PW // cols
    for dq, source in enumerate((near, far)):
        for d in range(cols):
            r = (my_a ^ d) * fan + (my_q ^ dq)
            pieces = [source[c ^ my_col, d, :held, :] for c in range(cols)]
            line = jnp.concatenate(
                [piece[:, k * col_share : (k + 1) * col_share] for k in range(NP) for piece in pieces],
                axis=1,
            )
            kids = []
            for e in range(cols):
                packed = source[e, d, held:, :]
                kids += [packed[:, :held], packed[:, held:]]
            kids = jnp.concatenate(kids, axis=0).T
            for k in range(NP):
                at = pl.ds(pl.multiple_of(k * PW + r * share, share), share)
                pile[at, :] = line[k * share : (k + 1) * share]
                wide[at, :] = kids[k * share : (k + 1) * share]
    piv[...] = wide[...].astype(BF16)
    piv_t[...] = wide[...].T.astype(BF16)
    product = dot(piv[...], piv_t[...])
    same_group = pivot_values(group_of, tiles, share, True) == pivot_values(group_of, tiles, share, False)
    same_kid = pivot_values(kid_of, tiles, share, True) == pivot_values(kid_of, tiles, share, False)
    pile[...] = jnp.where(same_group, pile[...], 0.0) + jnp.where(same_kid, product, 0.0)
    low_rows[...] = pile[PW:, :]
    upper[...] = jnp.zeros_like(upper)
    start_panel(work, diag_col, diag_row, pile[:PW, :PW])
    factor_panel(work, upper, 0, PW // BLK // 2)


def first_kernel(begun, begun_upper, diag_col, diag_row, low_rows,
                 lower, inv_hi, inv_lo, inv_t_hi, inv_t_lo, link_out, link_t, rest, work, upper):
    work[...] = begun[...]
    upper[...] = begun_upper[...]
    factor_panel(work, upper, PW // BLK // 2, PW // BLK)
    inverse = finish_panel(work, upper, diag_col, diag_row, lower, inv_hi, inv_lo, inv_t_hi, inv_t_lo)
    link = exact(low_rows[:, :PW], inverse, NT).astype(BF16)
    link_out[...] = link
    lower[PW:, :] = link.astype(F32)
    link_t[...] = link.astype(F32).T.astype(BF16)
    rest[...] = low_rows[:, PW:] - dot(link, link, NT)


def second_kernel(rest, lower, inv_hi, inv_lo, inv_t_hi, inv_t_lo, work, upper, diag_col, diag_row):
    start_panel(work, diag_col, diag_row, rest[...])
    factor_panel(work, upper, 0, PW // BLK)
    finish_panel(work, upper, diag_col, diag_row, lower, inv_hi, inv_lo, inv_t_hi, inv_t_lo)


def place_kernel(sizes, place, inverse_map, held, *outs):
    cols, fan, tiles, slice_cols = sizes
    my_row, my_col = place[0], place[1]
    my_q = my_row % fan

    def fetch(block, i):
        tile = inverse_map[block * tiles + i]
        at = pl.multiple_of((tile % tiles) * TS, TS)
        return held[tile // tiles, :, pl.ds(at, TS)]

    for i in range(tiles):
        mine = fetch(my_row, i)
        for d in range(cols):
            outs[d][:slice_cols, i * TS : (i + 1) * TS] = mine
    for d in range(cols):
        for i in range(tiles):
            outs[d][slice_cols:, i * TS : (i + 1) * TS] = fetch((my_col ^ d) * fan + my_q, i)


def together(*parts):
    parts = list(parts)
    while parts:
        for part in list(parts):
            try:
                next(part)
            except StopIteration:
                parts.remove(part)


def col_kernel(sizes, place, group_of, kid_of, strips, near_kids, far_kids,
               piv, inv1_hi, inv1_lo, inv2_hi, inv2_lo, link, out, strip, kids):
    rows, fan, share, block_cols, local_rows, tiles, wide = sizes
    my_row, my_col = place[0], place[1]
    my_q = my_row % fan
    j = pl.program_id(0)
    q = (j * block_cols) // local_rows
    group_col = pivot_values(group_of, tiles, share, True)
    kid_col = pivot_values(kid_of, tiles, share, True)

    @pl.when(q == my_q)
    def _():
        kids[...] = near_kids[...]

    @pl.when(q != my_q)
    def _():
        kids[...] = far_kids[...]

    def col_solve(n, pile):
        at = slice(n * wide, (n + 1) * wide)
        for r in range(rows):
            piece = strips[r, :, at].astype(F32)
            for k in range(NP):
                low = k * PW + r * share
                pile[low : low + share, :] = piece[k * share : (k + 1) * share]
        tile = my_col * fan * tiles + (j * block_cols + n * wide) // TS
        group_all = tile_values(group_of, tile, wide // TS)
        kid_all = tile_values(kid_of, tile, wide // TS)
        product = dot(piv[...], kids[:, at])
        yield
        full = jnp.where(group_col == group_all, pile[...], 0.0) + jnp.where(
            kid_col == kid_all, product, 0.0
        )
        first, second = full[:PW].astype(BF16), full[PW:]
        yield
        both = dot(jnp.concatenate([inv1_hi[...], inv1_lo[...]], axis=0), first)
        yield
        head = (both[:PW] + both[PW:]).astype(BF16)
        out[:PW, at] = -head
        yield
        second = (second - dot(link[...], head)).astype(BF16)
        yield
        both = dot(jnp.concatenate([inv2_hi[...], inv2_lo[...]], axis=0), second)
        yield
        out[PW:, at] = (-(both[:PW] + both[PW:])).astype(BF16)

    together(*[col_solve(n, strip.at[n]) for n in range(block_cols // wide)])


def schur_kernel(sizes, masks, place, group_of, kid_of,
                 piv_t, lower1, lower2, inv1_t_hi, inv1_t_lo, inv2_t_hi, inv2_t_lo, link_t, *refs):
    cols, fan, share, held, slice_cols, block_rows, local_rows, local_cols, tiles = sizes
    front, solved_cols, near_kids, far_kids = refs[:4]
    sources = refs[4 : 4 + cols]
    halves = [refs[4 + cols : 4 + 2 * cols], refs[4 + 2 * cols : 4 + 3 * cols]]
    out, panel = refs[4 + 3 * cols : 6 + 3 * cols]
    (fronts, outs, kids, own_t, pieces, flipped, solved_even, solved_odd, own_even, own_odd,
     front_sems, out_sems, flip_sem, kid_sems, own_sems, piece_sems) = refs[6 + 3 * cols :]
    my_row, my_col = place[0], place[1]
    my_q = my_row % fan
    first_tile = my_col * fan * tiles
    steps = local_rows // block_rows
    depth = fronts.shape[0] // 2
    half_rows = local_rows // 2

    def rows_at(i):
        return pl.ds(pl.multiple_of(i * block_rows, block_rows), block_rows)

    def front_copy(i, slot):
        return pltpu.make_async_copy(front.at[rows_at(i), :], fronts.at[slot], front_sems.at[slot])

    def out_copy(i, slot):
        return pltpu.make_async_copy(outs.at[slot], out.at[rows_at(i), :], out_sems.at[slot])

    kid_copies = [
        pltpu.make_async_copy(
            source,
            kids.at[:, pl.ds(pl.multiple_of((my_q ^ q) * local_rows, local_rows), local_rows)],
            kid_sems.at[q],
        )
        for q, source in enumerate((near_kids, far_kids))
    ]
    flip_copy = pltpu.make_async_copy(solved_cols, flipped, flip_sem)
    own_copies = [
        pltpu.make_async_copy(
            source.at[:slice_cols, :], own_t.at[d * slice_cols : (d + 1) * slice_cols, :], own_sems.at[d]
        )
        for d, source in enumerate(sources)
    ]
    piece_copies = [
        pltpu.make_async_copy(
            halves[half][i],
            pieces.at[my_col ^ mask, half * half_rows : (half + 1) * half_rows, :],
            piece_sems.at[half * cols + i],
        )
        for half in range(2)
        for i, mask in enumerate(masks[half])
    ]
    for copy in own_copies + piece_copies + [flip_copy] + kid_copies:
        copy.start()
    front_copy(0, 0).start()
    for copy in own_copies + piece_copies:
        copy.wait()
    col_share = PW // cols
    subs = block_rows // TS
    per_tile = 128 // col_share
    span = min(512, local_cols)
    group_row = pivot_values(group_of, tiles, share, False)
    kid_row = pivot_values(kid_of, tiles, share, False)
    lane = lax.broadcasted_iota(jnp.int32, (block_rows, 128), 1)

    def row_solve(step, opening, own_ref, solved):
        own = own_t[:, rows_at(step)].astype(F32).T.astype(BF16)
        own_ref[...] = own
        product = dot(own, piv_t[...])
        yield
        entries = jnp.concatenate(
            [
                pieces[c, rows_at(step), k * col_share : (k + 1) * col_share]
                for k in range(NP)
                for c in range(cols)
            ],
            axis=1,
        )
        my_tile = my_row * tiles + step * subs
        parts = []
        for i in range(subs):
            part = slice(i * TS, (i + 1) * TS)
            parts.append(
                jnp.where(group_row == group_of[my_tile + i], entries[part], 0.0)
                + jnp.where(kid_row == kid_of[my_tile + i], product[part], 0.0)
            )
        full = jnp.concatenate(parts, axis=0)
        high, low = split(full[:, :PW])
        yield
        head = dot(high, inv1_t_hi[...]) + dot(high, inv1_t_lo[...]) + dot(low, inv1_t_hi[...])
        solved[:, :PW] = head
        yield
        high, low = split(full[:, PW:] - dot(head.astype(BF16), link_t[...]))
        yield
        solved[:, PW:] = dot(high, inv2_t_hi[...]) + dot(high, inv2_t_lo[...]) + dot(low, inv2_t_hi[...])
        yield
        if opening:
            at = pl.multiple_of(my_row * share, share)
            solved[:share, :PW] = lower1[pl.ds(at, share), :]
            solved[:share, PW:] = jnp.zeros((share, PW), F32)
            solved[share : 2 * share, :PW] = lower1[pl.ds(PW + at, share), :]
            solved[share : 2 * share, PW:] = lower2[pl.ds(at, share), :]
        moved_out = jnp.zeros((block_rows, 128), F32)
        for k in range(NP):
            tile = pl.multiple_of(k * PW + (my_col // per_tile) * 128, 128)
            turn = (128 + k * col_share - (my_col % per_tile) * col_share) % 128
            moved = pltpu.roll(solved[:, pl.ds(tile, 128)], turn, 1)
            moved_out = jnp.where(lane // col_share == k, moved, moved_out)
        panel[rows_at(step), :] = moved_out[:, : NP * col_share].astype(BF16)

    def update(step, slot, own_ref, solved):
        lead, own = solved[...].astype(BF16), own_ref[...]
        my_tile = my_row * tiles + step * subs
        for n in range(local_cols // span):
            at = slice(n * span, (n + 1) * span)
            change = dot(lead, flipped[:, at])
            product = dot(own, kids[:, at])
            group_all = tile_values(group_of, first_tile + n * (span // TS), span // TS)
            kid_all = tile_values(kid_of, first_tile + n * (span // TS), span // TS)
            for i in range(subs):
                part = slice(i * TS, (i + 1) * TS)
                outs[slot, part, at] = (
                    jnp.where(group_all == group_of[my_tile + i], fronts[slot, part, at], 0.0)
                    + jnp.where(kid_all == kid_of[my_tile + i], product[part], 0.0)
                    + change[part]
                )
            yield

    together(row_solve(0, True, own_even, solved_even))
    for copy in [flip_copy] + kid_copies:
        copy.wait()
    for i in range(1, 2 * depth):
        front_copy(i, i).start()

    def two_blocks(pair, carry):
        for odd in range(2):
            step = 2 * pair + odd
            slot = 2 * lax.rem(pair, depth) + odd
            front_copy(step, slot).wait()

            @pl.when(pair >= depth)
            def _():
                out_copy(step - 2 * depth, slot).wait()

            if odd:
                mine, later = (own_odd, solved_odd), (own_even, solved_even)
            else:
                mine, later = (own_even, solved_even), (own_odd, solved_odd)
            together(update(step, slot, *mine), row_solve(jnp.minimum(step + 1, steps - 1), False, *later))
            for q in range(fan):
                outs[slot, :, q * local_rows : q * local_rows + held] = jnp.zeros((block_rows, held), F32)
            if not odd:

                @pl.when(pair == 0)
                def _():
                    outs[slot, :held, :] = jnp.zeros((held, local_cols), F32)

            out_copy(step, slot).start()

            @pl.when(pair + depth < steps // 2)
            def _():
                front_copy(step + 2 * depth, slot).start()

        return carry

    lax.fori_loop(0, steps // 2, two_blocks, 0)
    for i in range(steps - 2 * depth, steps):
        out_copy(i, i % (2 * depth)).wait()


def params():
    return pltpu.CompilerParams(vmem_limit_bytes=VMEM_BYTES)


def local(front_entries, tile_group, child_factor, row_map):
    rows, cols = lax.axis_size("row"), lax.axis_size("col")
    fan = rows // cols
    assert fan == 2
    local_rows, local_cols = front_entries.shape
    slice_cols = child_factor.shape[1]
    kid_cols = slice_cols * cols
    tiles = local_rows // TS
    share = PW // rows
    held = NP * share
    my_row, my_col = lax.axis_index("row"), lax.axis_index("col")
    place = jnp.stack([my_row, my_col]).astype(jnp.int32)

    flipped = child_factor.T
    own_map = lax.dynamic_slice_in_dim(row_map, my_row * tiles, tiles)
    starts = flipped.reshape(slice_cols, tiles, TS)[:, :, :held]

    def chosen(block):
        keep = (own_map == block * tiles)[None, :, None]
        return jnp.sum(jnp.where(keep, starts, 0), axis=1, dtype=F32)

    corner = jnp.concatenate(
        [
            front_entries[:held, q * local_rows + k * share : q * local_rows + (k + 1) * share]
            for k in range(NP)
            for q in range(fan)
        ],
        axis=1,
    )
    kids = jnp.concatenate([chosen(my_row), chosen(jnp.bitwise_xor(my_row, rows // 2))], axis=1)
    packet = jnp.concatenate([corner, kids], axis=0)
    packets = [swapped(packet, "row", d * fan) for d in range(cols)]

    row_strip = jnp.concatenate(
        [
            front_entries[:, q * local_rows + k * share : q * local_rows + (k + 1) * share]
            for k in range(NP)
            for q in range(fan)
        ],
        axis=1,
    )
    gathered = lax.all_gather(flipped, "row", axis=0)
    col_strip, row_strip, *packets = lax.optimization_barrier(
        (front_entries[:held].astype(BF16), row_strip, *packets)
    )
    col_strips = lax.all_gather(col_strip, "row", axis=0)
    steps = [1 << i for i in range(cols.bit_length() - 1)]
    orders = [steps, steps[::-1]]
    halves = [[row_strip[: local_rows // 2]], [row_strip[local_rows // 2 :]]]
    masks = [[0], [0]]

    def pass_on(halves, count, own_only):
        for h in range(2):
            for step in orders[h][:count]:
                for piece, mask in list(zip(halves[h], masks[h])):
                    if mask ^ step not in masks[h] and (mask == 0 or not own_only):
                        halves[h].append(swapped(piece, "col", step))
                        masks[h].append(mask ^ step)

    pass_on(halves, 1, True)
    merged = []
    for d in range(cols):
        kid = packets[d][held:, :held] + packets[d ^ (cols // 2)][held:, held:]
        half = slice_cols // 2
        merged.append(
            jnp.concatenate(
                [packets[d][:held], jnp.concatenate([kid[:half], kid[half:]], axis=1)], axis=0
            )
        )
    merged = jnp.stack(merged)
    near = jnp.stack([swapped(merged, "col", d) for d in range(cols)])
    far = swapped(near, "row", 1)

    tile_ids = jnp.arange(row_map.shape[0], dtype=jnp.int32)
    inverse_map = jnp.sum(
        jnp.where(row_map[None, :] == tile_ids[:, None], tile_ids[None, :], 0), axis=1, dtype=jnp.int32
    )
    kid_of = (inverse_map >= row_map.shape[0] // 2).astype(F32)
    group_of = jnp.repeat(tile_group, MT // TS).astype(F32)

    state = jax.ShapeDtypeStruct((PW, PW), F32)
    state_scratch = [pltpu.VMEM((PW, PW), F32), pltpu.VMEM((PW, PW), F32)]
    diag_scratch = [pltpu.VMEM((PW, 128), F32), pltpu.VMEM((8, PW), F32)]
    begun, begun_upper, diag_col, diag_row, low_rows, piv_t, piv = pl.pallas_call(
        functools.partial(open_kernel, (cols, fan, share, held, tiles)),
        out_shape=[
            state, state,
            jax.ShapeDtypeStruct((PW, 128), F32),
            jax.ShapeDtypeStruct((8, PW), F32),
            jax.ShapeDtypeStruct((PW, NPIV), F32),
            jax.ShapeDtypeStruct((kid_cols, NPIV), BF16),
            jax.ShapeDtypeStruct((NPIV, kid_cols), BF16),
        ],
        in_specs=[smem_spec()] * 3 + [whole_spec()] * 2,
        out_specs=[whole_spec()] * 7,
        scratch_shapes=[pltpu.VMEM((NPIV, NPIV), F32), pltpu.VMEM((NPIV, kid_cols), F32)],
        compiler_params=params(),
        cost_estimate=pl.CostEstimate(flops=10**10, bytes_accessed=3 * 10**7, transcendentals=0),
        name="open_pivots",
    )(place, group_of, kid_of, near, far)

    begun, gathered, halves[0][0], halves[1][0] = lax.optimization_barrier(
        (begun, gathered, halves[0][0], halves[1][0])
    )
    pass_on(halves, cols, True)
    placed = pl.pallas_call(
        functools.partial(place_kernel, (cols, fan, tiles, slice_cols)),
        out_shape=[jax.ShapeDtypeStruct((2 * slice_cols, local_rows), BF16)] * cols,
        in_specs=[smem_spec()] * 2 + [whole_spec()],
        out_specs=[whole_spec()] * cols,
        compiler_params=params(),
        cost_estimate=pl.CostEstimate(flops=0, bytes_accessed=2**16, transcendentals=0),
        name="place_tiles",
    )(place, inverse_map, gathered)
    begun, *placed = lax.optimization_barrier((begun, *placed))
    kid_parts = [swapped(placed[d], "col", d) for d in range(cols)]

    square = jax.ShapeDtypeStruct((PW, PW), BF16)
    lower1, inv1_hi, inv1_lo, inv1_t_hi, inv1_t_lo, link, link_t, rest = pl.pallas_call(
        first_kernel,
        out_shape=[
            jax.ShapeDtypeStruct((2 * PW, PW), F32),
            square, square, square, square, square, square, state,
        ],
        in_specs=[whole_spec()] * 5,
        out_specs=[whole_spec()] * 8,
        scratch_shapes=state_scratch,
        compiler_params=params(),
        cost_estimate=pl.CostEstimate(flops=10**9, bytes_accessed=10**6, transcendentals=0),
        name="first_pivots",
    )(begun, begun_upper, diag_col, diag_row, low_rows)
    lower2, inv2_hi, inv2_lo, inv2_t_hi, inv2_t_lo = pl.pallas_call(
        second_kernel,
        out_shape=[jax.ShapeDtypeStruct((PW, PW), F32), square, square, square, square],
        in_specs=[whole_spec()],
        out_specs=[whole_spec()] * 5,
        scratch_shapes=state_scratch + diag_scratch,
        compiler_params=params(),
        cost_estimate=pl.CostEstimate(flops=2 * 10**9, bytes_accessed=10**6, transcendentals=0),
        name="second_pivots",
    )(rest)

    lower2, kid_parts, halves = lax.optimization_barrier((lower2, kid_parts, halves))
    near_kids = jnp.concatenate([part[slice_cols:] for part in kid_parts], axis=0)
    far_kids = swapped(near_kids, "row", 1)
    pass_on(halves, cols, False)

    block_cols = min(1024, local_rows)
    per_block = local_rows // block_cols
    wide = min(512, block_cols)
    solved_cols = pl.pallas_call(
        functools.partial(col_kernel, (rows, fan, share, block_cols, local_rows, tiles, wide)),
        grid=(local_cols // block_cols,),
        out_shape=jax.ShapeDtypeStruct((NPIV, local_cols), BF16),
        in_specs=[smem_spec()] * 3
        + [
            pl.BlockSpec((rows, held, block_cols), lambda j: (0, 0, j)),
            pl.BlockSpec((kid_cols, block_cols), lambda j: (0, j % per_block)),
            pl.BlockSpec((kid_cols, block_cols), lambda j: (0, j % per_block)),
        ]
        + [whole_spec()] * 6,
        out_specs=pl.BlockSpec((NPIV, block_cols), lambda j: (0, j)),
        scratch_shapes=[
            pltpu.VMEM((block_cols // wide, NPIV, wide), F32),
            pltpu.VMEM((kid_cols, block_cols), BF16),
        ],
        compiler_params=params(),
        cost_estimate=pl.CostEstimate(flops=10**10, bytes_accessed=3 * 10**7, transcendentals=0),
        name="col_factors",
    )(
        place, group_of, kid_of, col_strips, near_kids, far_kids,
        piv, inv1_hi, inv1_lo, inv2_hi, inv2_lo, link,
    )

    block_rows = min(256, local_rows)
    depth = min(2, local_rows // block_rows // 2)
    schur_block, factor_panels = pl.pallas_call(
        functools.partial(
            schur_kernel,
            (cols, fan, share, held, slice_cols, block_rows, local_rows, local_cols, tiles),
            masks,
        ),
        out_shape=[
            jax.ShapeDtypeStruct((local_rows, local_cols), F32),
            jax.ShapeDtypeStruct((local_rows, NP * PW // cols), BF16),
        ],
        in_specs=[smem_spec()] * 3 + [whole_spec()] * 8 + [any_spec()] * (4 + 3 * cols),
        out_specs=[any_spec(), whole_spec()],
        scratch_shapes=[
            pltpu.VMEM((2 * depth, block_rows, local_cols), F32),
            pltpu.VMEM((2 * depth, block_rows, local_cols), F32),
            pltpu.VMEM((kid_cols, local_cols), BF16),
            pltpu.VMEM((kid_cols, local_rows), BF16),
            pltpu.VMEM((cols, local_rows, fan * held), F32),
            pltpu.VMEM((NPIV, local_cols), BF16),
            pltpu.VMEM((block_rows, NPIV), F32),
            pltpu.VMEM((block_rows, NPIV), F32),
            pltpu.VMEM((block_rows, kid_cols), BF16),
            pltpu.VMEM((block_rows, kid_cols), BF16),
            pltpu.SemaphoreType.DMA((2 * depth,)),
            pltpu.SemaphoreType.DMA((2 * depth,)),
            pltpu.SemaphoreType.DMA,
            pltpu.SemaphoreType.DMA((fan,)),
            pltpu.SemaphoreType.DMA((cols,)),
            pltpu.SemaphoreType.DMA((2 * cols,)),
        ],
        compiler_params=params(),
        cost_estimate=pl.CostEstimate(flops=3 * 10**10, bytes_accessed=9 * 10**7, transcendentals=0),
        name="schur_update",
    )(
        place, group_of, kid_of, piv_t, lower1, lower2,
        inv1_t_hi, inv1_t_lo, inv2_t_hi, inv2_t_lo, link_t,
        front_entries, solved_cols, near_kids, far_kids, *kid_parts,
        *halves[0], *halves[1],
    )
    return (factor_panels, schur_block)


def solution(mesh):
    placed = (P("row", "col"), P(), P("row", "col"), P())
    return jax.shard_map(
        local,
        mesh=mesh,
        in_specs=placed,
        out_specs=(P("row", "col"), P("row", "col")),
        check_vma=False,
    )
```

profile of v0, /device:TPU:0, one launch (start us, length us, event | category | flops | bytes accessed | tf_op | source)
XLA Modules:
  0.0 140.8 jit_solution(10245586549077625518)
XLA Ops:
  8.0 1.0 copy.6
  8.9 0.7 broadcast_compare_fusion
  10.1 0.9 fusion.1
  11.1 5.1 %collective-permute-start.2 = (f32[128,128]{1,0:T(8,128)S(1)}, f32[128,128]{1,0:T(8,128)S(1)}, u32[]{:S(2)}, u32[]{:S(2)}) collective-permute-start(f32[128,128]{1,0:T(8,128)S(1)} %maximum_maximum_fusion), channel_id=1, source_target_pairs={{0,24},{4,28},{8,16},{12,20},{16,8},{20,12},{24,0},{28,4},{1,25},{... | collective-permute-start | bytes 196616 | tf_op jit(solution)/shard_map/ppermute | solution.py:41
  16.9 2.9 %fusion.2 = (f32[2048,32]{1,0:T(8,128)S(1)}, f32[2048,32]{1,0:T(8,128)S(1)}, f32[2048,32]{1,0:T(8,128)S(1)}, f32[2048,32]{1,0:T(8,128)S(1)}) fusion(f32[2048,4096]{1,0:T(8,128)} %refs_0_.1), kind=kLoop, calls=%fused_computation.24 | loop fusion | bytes 2097152 | tf_op jit(solution)/shard_map/slice | solution.py:504
  19.8 0.9 pad_maximum_fusion
  20.7 2.1 %slice.166 = bf16[64,4096]{1,0:T(8,128)(2,1)} slice(f32[2048,4096]{1,0:T(8,128)} %refs_0_.1), slice={[0:64], [0:4096]} | slice | bytes 1048576 | tf_op jit(solution)/shard_map/slice | solution.py:512
  23.4 1.7 %collective-permute-start.4 = (f32[4,96,128]{2,1,0:T(8,128)S(1)}, f32[4,96,128]{2,1,0:T(8,128)S(1)}, u32[]{:S(2)}, u32[]{:S(2)}) collective-permute-start(f32[4,96,128]{2,1,0:T(8,128)S(1)} %get-tuple-element.119), channel_id=1, source_target_pairs={{0,2},{1,3},{2,0},{3,1},{4,6},{5,7},{6,4},{7,5},{8,10},{9,11},{10,... | collective-permute-start | bytes 589832 | tf_op jit(solution)/shard_map/ppermute | solution.py:41
  25.1 1.5 %collective-permute-start.3 = (f32[4,96,128]{2,1,0:T(8,128)S(1)}, f32[4,96,128]{2,1,0:T(8,128)S(1)}, u32[]{:S(2)}, u32[]{:S(2)}) collective-permute-start(f32[4,96,128]{2,1,0:T(8,128)S(1)} %get-tuple-element.119), channel_id=1, source_target_pairs={{0,1},{1,0},{2,3},{3,2},{4,5},{5,4},{6,7},{7,6},{8,9},{9,8},{10,11... | collective-permute-start | bytes 589832 | tf_op jit(solution)/shard_map/ppermute | solution.py:41
  26.9 3.4 %collective-permute-done.4 = f32[4,96,128]{2,1,0:T(8,128)S(1)} collective-permute-done((f32[4,96,128]{2,1,0:T(8,128)S(1)}, f32[4,96,128]{2,1,0:T(8,128)S(1)}, u32[]{:S(2)}, u32[]{:S(2)}) %collective-permute-start.4) | collective-permute-done | bytes 196640 | tf_op jit(solution)/shard_map/ppermute | solution.py:41
  30.4 2.5 %collective-permute-done.3 = f32[4,96,128]{2,1,0:T(8,128)S(1)} collective-permute-done((f32[4,96,128]{2,1,0:T(8,128)S(1)}, f32[4,96,128]{2,1,0:T(8,128)S(1)}, u32[]{:S(2)}, u32[]{:S(2)}) %collective-permute-start.3) | collective-permute-done | bytes 196640 | tf_op jit(solution)/shard_map/ppermute | solution.py:41
  32.8 2.2 %collective-permute-done.5 = f32[4,96,128]{2,1,0:T(8,128)S(1)} collective-permute-done((f32[4,96,128]{2,1,0:T(8,128)S(1)}, f32[4,96,128]{2,1,0:T(8,128)S(1)}, u32[]{:S(2)}, u32[]{:S(2)}) %collective-permute-start.5) | collective-permute-done | bytes 196640 | tf_op jit(solution)/shard_map/ppermute | solution.py:41
  35.2 0.7 convert_element_type.19.group_of
  37.2 1.5 %collective-permute-start.12 = (f32[1024,128]{1,0:T(8,128)S(1)}, f32[1024,128]{1,0:T(8,128)S(1)}, u32[]{:S(2)}, u32[]{:S(2)}) collective-permute-start(f32[1024,128]{1,0:T(8,128)S(1)} %get-tuple-element.101.refs_12_), channel_id=1, source_target_pairs={{0,2},{1,3},{2,0},{3,1},{4,6},{5,7},{6,4},{7,5},{8,10},{9,11},{10,... | collective-permute-start | bytes 1572872 | tf_op jit(solution)/shard_map/ppermute | solution.py:41
  38.7 1.5 %collective-permute-start.10 = (f32[1024,128]{1,0:T(8,128)S(1)}, f32[1024,128]{1,0:T(8,128)S(1)}, u32[]{:S(2)}, u32[]{:S(2)}) collective-permute-start(f32[1024,128]{1,0:T(8,128)S(1)} %get-tuple-element.98.refs_8_), channel_id=1, source_target_pairs={{0,1},{1,0},{2,3},{3,2},{4,5},{5,4},{6,7},{7,6},{8,9},{9,8},{10,11... | collective-permute-start | bytes 1572872 | tf_op jit(solution)/shard_map/ppermute | solution.py:41
  40.2 9.2 %open_pivots.1 = (f32[256,256]{1,0:T(8,128)}, f32[256,256]{1,0:T(8,128)}, f32[256,128]{1,0:T(8,128)}, f32[8,256]{1,0:T(8,128)}, f32[256,512]{1,0:T(8,128)}, /*in...) custom-call(s32[2]{0:T(128)} %pad_add_fusion.place, f32[128]{0:T(128)} %convert_element_type.19.group_of, ...), custom_call_target="tpu_custom_call" | custom-call | flops 10000000000 | bytes 30000000 | tf_op jit(solution)/shard_map/open_pivots/pallas_call | solution.py:552
  50.6 3.8 %place_tiles.1 = (bf16[128,2048]{1,0:T(8,128)(2,1)}, bf16[128,2048]{1,0:T(8,128)(2,1)}, bf16[128,2048]{1,0:T(8,128)(2,1)}, bf16[128,2048]{1,0:T(8,128)(2,1)}) custom-call(s32[2]{0:T(128)} %pad_add_fusion.place, s32[128]{0:T(128)} %copy-done.9, bf16[8,64,2048]{2,1,0:T(8,128)(2,1)} %bitcast.20), custom_call_target="tpu_custom_call" | custom-call | bytes 65536 | tf_op jit(solution)/shard_map/place_tiles/pallas_call | solution.py:574
  54.4 1.6 %collective-permute-start.7 = (bf16[128,2048]{1,0:T(8,128)(2,1)}, bf16[128,2048]{1,0:T(8,128)(2,1)S(1)}, u32[]{:S(2)}, u32[]{:S(2)}) collective-permute-start(bf16[128,2048]{1,0:T(8,128)(2,1)} %get-tuple-element.76), channel_id=1, source_target_pairs={{0,1},{1,0},{2,3},{3,2},{4,5},{5,4},{6,7},{7,6},{8,9},{9,8},{10,11... | collective-permute-start | bytes 1572872 | tf_op jit(solution)/shard_map/ppermute | solution.py:41
  56.0 1.5 %collective-permute-start.8 = (bf16[128,2048]{1,0:T(8,128)(2,1)}, bf16[128,2048]{1,0:T(8,128)(2,1)S(1)}, u32[]{:S(2)}, u32[]{:S(2)}) collective-permute-start(bf16[128,2048]{1,0:T(8,128)(2,1)} %get-tuple-element.77), channel_id=1, source_target_pairs={{0,2},{1,3},{2,0},{3,1},{4,6},{5,7},{6,4},{7,5},{8,10},{9,11},{10,... | collective-permute-start | bytes 1572872 | tf_op jit(solution)/shard_map/ppermute | solution.py:41
  57.5 0.8 collective-permute-start.9
  58.3 8.7 %first_pivots.1 = (f32[512,256]{1,0:T(8,128)}, bf16[256,256]{1,0:T(8,128)(2,1)}, bf16[256,256]{1,0:T(8,128)(2,1)}, bf16[256,256]{1,0:T(8,128)(2,1)}, bf16[256,25...) custom-call(f32[256,256]{1,0:T(8,128)} %get-tuple-element.67.begun, ...), custom_call_target="tpu_custom_call" | custom-call | flops 1000000000 | bytes 1000000 | tf_op jit(solution)/shard_map/first_pivots/pallas_call | solution.py:587
  66.9 13.7 %second_pivots.1 = (f32[256,256]{1,0:T(8,128)}, bf16[256,256]{1,0:T(8,128)(2,1)}, bf16[256,256]{1,0:T(8,128)(2,1)}, bf16[256,256]{1,0:T(8,128)(2,1)}, bf16[256,256]{1,0:T(8,128)(2,1)}) custom-call(f32[256,256]{1,0:T(8,128)} %get-tuple-element.73.rest), custom_call_target="tpu_custom_call" | custom-call | flops 2000000000 | bytes 1000000 | tf_op jit(solution)/shard_map/second_pivots/pallas_call | solution.py:600
  80.7 6.2 %collective-permute-done.9.refs_7_ = bf16[128,2048]{1,0:T(8,128)(2,1)S(1)} collective-permute-done((bf16[128,2048]{1,0:T(8,128)(2,1)}, bf16[128,2048]{1,0:T(8,128)(2,1)S(1)}, u32[]{:S(2)}, u32[]{:S(2)}) %collective-permute-start.9) | collective-permute-done | bytes 524320 | tf_op jit(solution)/shard_map/ppermute | solution.py:41
  86.9 0.7 copy-done.7
  87.9 1.1 collective-permute-start.15
  88.9 1.5 %collective-permute-start.16 = (f32[1024,128]{1,0:T(8,128)}, f32[1024,128]{1,0:T(8,128)S(1)}, u32[]{:S(2)}, u32[]{:S(2)}) collective-permute-start(f32[1024,128]{1,0:T(8,128)} %collective-permute-done.13.refs_14_), channel_id=1, source_target_pairs={{0,2},{1,3},{2,0},{3,1},{4,6},{5,7},{6,4},{7,5},{8,10},{9,11},{10,... | collective-permute-start | bytes 1572872 | tf_op jit(solution)/shard_map/ppermute | solution.py:41
  90.5 1.0 copy-done.10
  91.5 9.1 %col_factors.1.refs_1_ = bf16[512,4096]{1,0:T(8,128)(2,1)} custom-call(s32[2]{0:T(128)} %pad_add_fusion.place, f32[128]{0:T(128)} %convert_element_type.19.group_of, f32[128]{0:T(128)} %compare_convert_fusion.kid_of, bf16[8,64,4096]{2,1,0:T(8,128)(2,1)} %bitcast.27, bf16[256,2048]{1,0:T(8,128)(2,1)} %copy-done, bf16[256,2048]{1,0:T(8,128)(2,1)} %copy-done.10, ...), custom_call_target="tpu_custom_call" | custom-call | flops 10000000000 | bytes 30000000 | tf_op jit(solution)/shard_map/col_factors/pallas_call | solution.py:619
  100.6 1.8 %collective-permute-done.15.refs_11_ = f32[1024,128]{1,0:T(8,128)S(1)} collective-permute-done((f32[1024,128]{1,0:T(8,128)}, f32[1024,128]{1,0:T(8,128)S(1)}, u32[]{:S(2)}, u32[]{:S(2)}) %collective-permute-start.15) | collective-permute-done | bytes 524320 | tf_op jit(solution)/shard_map/ppermute | solution.py:41
  102.4 0.7 collective-permute-done.16.refs_15_
  103.2 0.7 copy-done.14
  104.0 29.9 %schur_update.1 = (f32[2048,4096]{1,0:T(8,128)}, bf16[2048,128]{1,0:T(8,128)(2,1)}) custom-call(s32[2]{0:T(128)} %pad_add_fusion.place, f32[128]{0:T(128)} %convert_element_type.19.group_of, f32[128]{0:T(128)} %compare_convert_fusion.kid_of, bf16[256,512]{1,0:T(8,128)(2,1)} %get-tuple-element.58.piv_t, f32[512,256]{1,0:T(8,128)} %get-tuple-element.72.lower1, ...), custom_call_target="tpu_custom_call" | custom-call | flops 30000001024 | bytes 90000000 | tf_op jit(solution)/shard_map/schur_update/pallas_call | solution.py:645
  (81 shorter events, 5.9 us)
Async XLA Ops:
  7.2 42.2 %all-gather.5.cloned.1.call-start = ((), (), s32[]{:S(2)}) async-start(), calls=%async_computation | async-start | bytes 2359296 | tf_op jit(solution)/shard_map/all_gather | solution.py:510
  7.9 82.6 %all-gather.7.cloned.1.call-start = ((), (), s32[]{:S(2)}) async-start(), calls=%async_computation.1 | async-start | bytes 4718592 | tf_op jit(solution)/shard_map/all_gather | solution.py:514
  11.1 11.7 %collective-permute-start.2 = (f32[128,128]{1,0:T(8,128)S(1)}, f32[128,128]{1,0:T(8,128)S(1)}, u32[]{:S(2)}, u32[]{:S(2)}) collective-permute-start(f32[128,128]{1,0:T(8,128)S(1)} %maximum_maximum_fusion), channel_id=1, source_target_pairs={{0,24},{4,28},{8,16},{12,20},{16,8},{20,12},{24,0},{28,4},{1,25},{... | collective-permute-start | bytes 196616 | tf_op jit(solution)/shard_map/ppermute | solution.py:41
  16.2 6.6 %collective-permute-start.1 = (f32[128,128]{1,0:T(8,128)S(1)}, f32[128,128]{1,0:T(8,128)S(1)}, u32[]{:S(2)}, u32[]{:S(2)}) collective-permute-start(f32[128,128]{1,0:T(8,128)S(1)} %maximum_maximum_fusion), channel_id=1, source_target_pairs={{0,16},{4,20},{8,24},{12,28},{16,0},{20,4},{24,8},{28,12},{1,17},{... | collective-permute-start | bytes 196616 | tf_op jit(solution)/shard_map/ppermute | solution.py:41
  16.2 6.6 %collective-permute-start = (f32[128,128]{1,0:T(8,128)S(1)}, f32[128,128]{1,0:T(8,128)S(1)}, u32[]{:S(2)}, u32[]{:S(2)}) collective-permute-start(f32[128,128]{1,0:T(8,128)S(1)} %maximum_maximum_fusion), channel_id=1, source_target_pairs={{0,8},{4,12},{8,0},{12,4},{16,24},{20,28},{24,16},{28,20},{1,9},{5... | collective-permute-start | bytes 196616 | tf_op jit(solution)/shard_map/ppermute | solution.py:41
  22.8 12.4 %copy-start.15 = (s32[32]{0:T(128)S(1)}, s32[32]{0:T(128)}, u32[]{:S(2)}) copy-start(s32[32]{0:T(128)} %param.5) | copy-start | bytes 388
  22.8 13.7 %copy-start.8 = (s32[128]{0:T(128)S(1)}, s32[128]{0:T(128)}, u32[]{:S(2)}) copy-start(s32[128]{0:T(128)} %param.7) | copy-start | bytes 1540
  23.4 7.0 %collective-permute-start.4 = (f32[4,96,128]{2,1,0:T(8,128)S(1)}, f32[4,96,128]{2,1,0:T(8,128)S(1)}, u32[]{:S(2)}, u32[]{:S(2)}) collective-permute-start(f32[4,96,128]{2,1,0:T(8,128)S(1)} %get-tuple-element.119), channel_id=1, source_target_pairs={{0,2},{1,3},{2,0},{3,1},{4,6},{5,7},{6,4},{7,5},{8,10},{9,11},{10,... | collective-permute-start | bytes 589832 | tf_op jit(solution)/shard_map/ppermute | solution.py:41
  25.1 7.7 %collective-permute-start.3 = (f32[4,96,128]{2,1,0:T(8,128)S(1)}, f32[4,96,128]{2,1,0:T(8,128)S(1)}, u32[]{:S(2)}, u32[]{:S(2)}) collective-permute-start(f32[4,96,128]{2,1,0:T(8,128)S(1)} %get-tuple-element.119), channel_id=1, source_target_pairs={{0,1},{1,0},{2,3},{3,2},{4,5},{5,4},{6,7},{7,6},{8,9},{9,8},{10,11... | collective-permute-start | bytes 589832 | tf_op jit(solution)/shard_map/ppermute | solution.py:41
  26.6 8.4 %collective-permute-start.5 = (f32[4,96,128]{2,1,0:T(8,128)S(1)}, f32[4,96,128]{2,1,0:T(8,128)S(1)}, u32[]{:S(2)}, u32[]{:S(2)}) collective-permute-start(f32[4,96,128]{2,1,0:T(8,128)S(1)} %get-tuple-element.119), channel_id=1, source_target_pairs={{0,3},{1,2},{2,1},{3,0},{4,7},{5,6},{6,5},{7,4},{8,11},{9,10},{10,... | collective-permute-start | bytes 589832 | tf_op jit(solution)/shard_map/ppermute | solution.py:41
  35.1 5.1 %copy-start.1 = (f32[4,4,96,128]{3,2,1,0:T(8,128)}, f32[4,4,96,128]{3,2,1,0:T(8,128)S(1)}, u32[]{:S(2)}) copy-start(f32[4,4,96,128]{3,2,1,0:T(8,128)S(1)} %pad_maximum_fusion.2.near) | copy-start | bytes 2359300
  35.1 5.1 %collective-permute-start.6 = (f32[4,4,96,128]{3,2,1,0:T(8,128)S(1)}, f32[4,4,96,128]{3,2,1,0:T(8,128)}, u32[]{:S(2)}, u32[]{:S(2)}) collective-permute-start(f32[4,4,96,128]{3,2,1,0:T(8,128)S(1)} %pad_maximum_fusion.2.near), channel_id=1, source_target_pairs={{0,4},{4,0},{8,12},{12,8},{16,20},{20,16},{24,28},{28,24},{1,5},{5... | collective-permute-start | bytes 2359304 | tf_op jit(solution)/shard_map/ppermute | solution.py:41
  36.6 12.8 %copy-start.9 = (s32[128]{0:T(128)}, s32[128]{0:T(128)S(1)}, u32[]{:S(2)}) copy-start(s32[128]{0:T(128)S(1)} %select_reduce_fusion.inverse_map) | copy-start | bytes 1540
  37.2 12.2 %copy-start.3 = (f32[1024,128]{1,0:T(8,128)}, f32[1024,128]{1,0:T(8,128)S(1)}, u32[]{:S(2)}) copy-start(f32[1024,128]{1,0:T(8,128)S(1)} %get-tuple-element.98.refs_8_) | copy-start | bytes 1572868
  37.2 12.8 %copy-start.2 = (f32[1024,128]{1,0:T(8,128)}, f32[1024,128]{1,0:T(8,128)S(1)}, u32[]{:S(2)}) copy-start(f32[1024,128]{1,0:T(8,128)S(1)} %get-tuple-element.101.refs_12_) | copy-start | bytes 1572868
  37.2 18.7 %collective-permute-start.12 = (f32[1024,128]{1,0:T(8,128)S(1)}, f32[1024,128]{1,0:T(8,128)S(1)}, u32[]{:S(2)}, u32[]{:S(2)}) collective-permute-start(f32[1024,128]{1,0:T(8,128)S(1)} %get-tuple-element.101.refs_12_), channel_id=1, source_target_pairs={{0,2},{1,3},{2,0},{3,1},{4,6},{5,7},{6,4},{7,5},{8,10},{9,11},{10,... | collective-permute-start | bytes 1572872 | tf_op jit(solution)/shard_map/ppermute | solution.py:41
  38.7 18.8 %collective-permute-start.10 = (f32[1024,128]{1,0:T(8,128)S(1)}, f32[1024,128]{1,0:T(8,128)S(1)}, u32[]{:S(2)}, u32[]{:S(2)}) collective-permute-start(f32[1024,128]{1,0:T(8,128)S(1)} %get-tuple-element.98.refs_8_), channel_id=1, source_target_pairs={{0,1},{1,0},{2,3},{3,2},{4,5},{5,4},{6,7},{7,6},{8,9},{9,8},{10,11... | collective-permute-start | bytes 1572872 | tf_op jit(solution)/shard_map/ppermute | solution.py:41
  49.4 31.3 %collective-permute-start.11 = (f32[1024,128]{1,0:T(8,128)S(1)}, f32[1024,128]{1,0:T(8,128)}, u32[]{:S(2)}, u32[]{:S(2)}) collective-permute-start(f32[1024,128]{1,0:T(8,128)S(1)} %get-tuple-element.98.refs_8_), channel_id=1, source_target_pairs={{0,2},{1,3},{2,0},{3,1},{4,6},{5,7},{6,4},{7,5},{8,10},{9,11},{10,... | collective-permute-start | bytes 1572872 | tf_op jit(solution)/shard_map/ppermute | solution.py:41
  50.0 30.7 %collective-permute-start.13 = (f32[1024,128]{1,0:T(8,128)S(1)}, f32[1024,128]{1,0:T(8,128)}, u32[]{:S(2)}, u32[]{:S(2)}) collective-permute-start(f32[1024,128]{1,0:T(8,128)S(1)} %get-tuple-element.101.refs_12_), channel_id=1, source_target_pairs={{0,1},{1,0},{2,3},{3,2},{4,5},{5,4},{6,7},{7,6},{8,9},{9,8},{10,11... | collective-permute-start | bytes 1572872 | tf_op jit(solution)/shard_map/ppermute | solution.py:41
  54.4 26.3 %collective-permute-start.7 = (bf16[128,2048]{1,0:T(8,128)(2,1)}, bf16[128,2048]{1,0:T(8,128)(2,1)S(1)}, u32[]{:S(2)}, u32[]{:S(2)}) collective-permute-start(bf16[128,2048]{1,0:T(8,128)(2,1)} %get-tuple-element.76), channel_id=1, source_target_pairs={{0,1},{1,0},{2,3},{3,2},{4,5},{5,4},{6,7},{7,6},{8,9},{9,8},{10,11... | collective-permute-start | bytes 1572872 | tf_op jit(solution)/shard_map/ppermute | solution.py:41
  56.0 1.5 %copy-start.11 = (f32[1024,128]{1,0:T(8,128)}, f32[1024,128]{1,0:T(8,128)S(1)}, u32[]{:S(2)}) copy-start(f32[1024,128]{1,0:T(8,128)S(1)} %collective-permute-done.12.refs_13_) | copy-start | bytes 1572868
  56.0 24.7 %collective-permute-start.8 = (bf16[128,2048]{1,0:T(8,128)(2,1)}, bf16[128,2048]{1,0:T(8,128)(2,1)S(1)}, u32[]{:S(2)}, u32[]{:S(2)}) collective-permute-start(bf16[128,2048]{1,0:T(8,128)(2,1)} %get-tuple-element.77), channel_id=1, source_target_pairs={{0,2},{1,3},{2,0},{3,1},{4,6},{5,7},{6,4},{7,5},{8,10},{9,11},{10,... | collective-permute-start | bytes 1572872 | tf_op jit(solution)/shard_map/ppermute | solution.py:41
  57.5 23.2 %copy-start.12 = (f32[1024,128]{1,0:T(8,128)}, f32[1024,128]{1,0:T(8,128)S(1)}, u32[]{:S(2)}) copy-start(f32[1024,128]{1,0:T(8,128)S(1)} %collective-permute-done.10.refs_9_) | copy-start | bytes 1572868
  57.5 29.4 %collective-permute-start.9 = (bf16[128,2048]{1,0:T(8,128)(2,1)}, bf16[128,2048]{1,0:T(8,128)(2,1)S(1)}, u32[]{:S(2)}, u32[]{:S(2)}) collective-permute-start(bf16[128,2048]{1,0:T(8,128)(2,1)} %get-tuple-element.78), channel_id=1, source_target_pairs={{0,3},{1,2},{2,1},{3,0},{4,7},{5,6},{6,5},{7,4},{8,11},{9,10},{10,... | collective-permute-start | bytes 1572872 | tf_op jit(solution)/shard_map/ppermute | solution.py:41
  66.9 19.9 %copy-start.4 = (bf16[128,2048]{1,0:T(8,128)(2,1)S(1)}, bf16[128,2048]{1,0:T(8,128)(2,1)}, u32[]{:S(2)}) copy-start(bf16[128,2048]{1,0:T(8,128)(2,1)} %get-tuple-element.88.refs_4_) | copy-start | bytes 1572868
  80.7 7.1 %copy-start.5 = (bf16[128,2048]{1,0:T(8,128)(2,1)}, bf16[128,2048]{1,0:T(8,128)(2,1)S(1)}, u32[]{:S(2)}) copy-start(bf16[128,2048]{1,0:T(8,128)(2,1)S(1)} %collective-permute-done.7.refs_5_) | copy-start | bytes 1572868
  80.7 7.1 %copy-start.6 = (bf16[128,2048]{1,0:T(8,128)(2,1)}, bf16[128,2048]{1,0:T(8,128)(2,1)S(1)}, u32[]{:S(2)}) copy-start(bf16[128,2048]{1,0:T(8,128)(2,1)S(1)} %collective-permute-done.8.refs_6_) | copy-start | bytes 1572868
  87.8 2.8 %copy-start = (bf16[256,2048]{1,0:T(8,128)(2,1)}, bf16[256,2048]{1,0:T(8,128)(2,1)S(1)}, u32[]{:S(2)}) copy-start(bf16[256,2048]{1,0:T(8,128)(2,1)S(1)} %pad_maximum_fusion.1.near_kids.refs_2_) | copy-start | bytes 3145732
  87.8 2.7 %collective-permute-start.14 = (bf16[256,2048]{1,0:T(8,128)(2,1)S(1)}, bf16[256,2048]{1,0:T(8,128)(2,1)S(1)}, u32[]{:S(2)}, u32[]{:S(2)}) collective-permute-start(bf16[256,2048]{1,0:T(8,128)(2,1)S(1)} %pad_maximum_fusion.1.near_kids.refs_2_), channel_id=1, source_target_pairs={{0,4},{4,0},{8,12},{12,8},{16,20},{20,16},{24,28},{28,24},{1,5},{5... | collective-permute-start | bytes 3145736 | tf_op jit(solution)/shard_map/ppermute | solution.py:41
  87.9 14.6 %collective-permute-start.15 = (f32[1024,128]{1,0:T(8,128)}, f32[1024,128]{1,0:T(8,128)S(1)}, u32[]{:S(2)}, u32[]{:S(2)}) collective-permute-start(f32[1024,128]{1,0:T(8,128)} %collective-permute-done.11.refs_10_), channel_id=1, source_target_pairs={{0,1},{1,0},{2,3},{3,2},{4,5},{5,4},{6,7},{7,6},{8,9},{9,8},{10,11... | collective-permute-start | bytes 1572872 | tf_op jit(solution)/shard_map/ppermute | solution.py:41
  88.9 14.2 %collective-permute-start.16 = (f32[1024,128]{1,0:T(8,128)}, f32[1024,128]{1,0:T(8,128)S(1)}, u32[]{:S(2)}, u32[]{:S(2)}) collective-permute-start(f32[1024,128]{1,0:T(8,128)} %collective-permute-done.13.refs_14_), channel_id=1, source_target_pairs={{0,2},{1,3},{2,0},{3,1},{4,6},{5,7},{6,4},{7,5},{8,10},{9,11},{10,... | collective-permute-start | bytes 1572872 | tf_op jit(solution)/shard_map/ppermute | solution.py:41
  90.5 1.0 copy-start.10
  (3 other events, 2.4 us)
Sparse Core Ops, SparseCore 0:
  9.6 31.7 all-gather.4
  43.0 47.4 all-gather.6
where the time goes:
time: 141 us
  Pallas kernels  74.3 us (53%)
  starting transfers between devices  20.2 us (14%)
  waiting for transfers between devices  17.6 us (12%)
  between operations  14.4 us (10%)
  local copies, waits for them, and re-layouts  10.5 us (7%)
  other arithmetic  3.86 us (3%)
    pallas_call x1, Pallas kernels, local(): pl.pallas_call(functools.partial(schur_kernel, (cols, fan, share, held, s...  29.9 us
    ppermute x17, starting transfers between devices, swapped(): lax.ppermute(value, axis, [(i, i ^ mask) for i in range(lax.axis_size(axi...  20.1 us
    ppermute x17, waiting for transfers between devices, swapped(): lax.ppermute(value, axis, [(i, i ^ mask) for i in range(lax.axis_size(axi...  16.9 us
    pallas_call x1, Pallas kernels, local(): pl.pallas_call(second_kernel, out_shape=[jax.ShapeDtypeStruct((PW, PW), F...  13.7 us
    pallas_call x1, Pallas kernels, local(): pl.pallas_call(functools.partial(open_kernel, (cols, fan, share, held, ti...  9.2 us
    pallas_call x1, Pallas kernels, local(): pl.pallas_call(functools.partial(col_kernel, (rows, fan, share, block_col...  9.07 us
    pallas_call x1, Pallas kernels, local(): pl.pallas_call(first_kernel, out_shape=[jax.ShapeDtypeStruct((2 * PW, PW)...  8.65 us
    pallas_call x1, Pallas kernels, local(): pl.pallas_call(functools.partial(place_kernel, (cols, fan, tiles, slice_c...  3.75 us
  transfers between devices with their start and end apart: 19, of which 7 were waited for; matrix products, arithmetic and copies ran while one was open for 8% of the time, Pallas kernels for 32%

commit v1 on v0

--- a/solution.py
+++ b/solution.py
@@ -508,9 +508,7 @@
         axis=1,
     )
     gathered = lax.all_gather(flipped, "row", axis=0)
-    col_strip, row_strip, *packets = lax.optimization_barrier(
-        (front_entries[:held].astype(BF16), row_strip, *packets)
-    )
+    col_strip, *packets = lax.optimization_barrier((front_entries[:held].astype(BF16), *packets))
     col_strips = lax.all_gather(col_strip, "row", axis=0)
     steps = [1 << i for i in range(cols.bit_length() - 1)]
     orders = [steps, steps[::-1]]

time: 141 us -> 142 us (level)
  starting transfers between devices: 20.2 us -> 18.3 us
  waiting for transfers between devices: 17.6 us -> 19.1 us
    ppermute x17, starting transfers between devices: 20.1 us -> 18.2 us  [swapped(): lax.ppermute(value, axis, [(i, i ^ mask) for i in range(lax.axis_size(axi...]
    ppermute x17, waiting for transfers between devices: 16.9 us -> 18.4 us  [swapped(): lax.ppermute(value, axis, [(i, i ^ mask) for i in range(lax.axis_size(axi...]
  transfers between devices with their start and end apart: 19 -> 19, of which waited for: 7 -> 8; matrix products, arithmetic and copies ran while one was open for 8% -> 8% of each run, Pallas kernels for 32% -> 31%
where the time goes in v1:
time: 142 us; the launch traced here: 141 us
  Pallas kernels  74.1 us (52%)
  waiting for transfers between devices  19.1 us (13%)
  starting transfers between devices  18.3 us (13%)
  between operations  14.4 us (10%)
  local copies, waits for them, and re-layouts  11.4 us (8%)
  other arithmetic  4.02 us (3%)
    pallas_call x1, Pallas kernels, local(): pl.pallas_call(functools.partial(schur_kernel, (cols, fan, share, held, s...  29.9 us
    ppermute x17, waiting for transfers between devices, swapped(): lax.ppermute(value, axis, [(i, i ^ mask) for i in range(lax.axis_size(axi...  18.4 us
    ppermute x17, starting transfers between devices, swapped(): lax.ppermute(value, axis, [(i, i ^ mask) for i in range(lax.axis_size(axi...  18.2 us
    pallas_call x1, Pallas kernels, local(): pl.pallas_call(second_kernel, out_shape=[jax.ShapeDtypeStruct((PW, PW), F...  13.7 us
    pallas_call x1, Pallas kernels, local(): pl.pallas_call(functools.partial(open_kernel, (cols, fan, share, held, ti...  9.19 us
    pallas_call x1, Pallas kernels, local(): pl.pallas_call(functools.partial(col_kernel, (rows, fan, share, block_col...  9.08 us
    pallas_call x1, Pallas kernels, local(): pl.pallas_call(first_kernel, out_shape=[jax.ShapeDtypeStruct((2 * PW, PW)...  8.59 us
    unnamed x33, local copies, waits for them, and re-layouts  4.64 us
  transfers between devices with their start and end apart: 19, of which 8 were waited for; matrix products, arithmetic and copies ran while one was open for 8% of the time, Pallas kernels for 31%

profile of v1, /device:TPU:0, one launch (start us, length us, event | category | flops | bytes accessed | tf_op | source)
XLA Modules:
  0.0 141.3 jit_solution(8204046070960099271)
XLA Ops:
  7.2 0.7 all-gather.5.cloned.1.call-update
  8.0 1.0 copy.6
  8.9 0.7 broadcast_compare_fusion
  10.1 0.9 fusion.2
  11.1 5.1 %collective-permute-start.2 = (f32[128,128]{1,0:T(8,128)S(1)}, f32[128,128]{1,0:T(8,128)S(1)}, u32[]{:S(2)}, u32[]{:S(2)}) collective-permute-start(f32[128,128]{1,0:T(8,128)S(1)} %maximum_maximum_fusion), channel_id=1, source_target_pairs={{0,24},{4,28},{8,16},{12,20},{16,8},{20,12},{24,0},{28,4},{1,25},{... | collective-permute-start | bytes 196616 | tf_op jit(solution)/shard_map/ppermute | solution.py:41
  16.2 0.6 collective-permute-start
  16.9 2.1 %slice.168 = bf16[64,4096]{1,0:T(8,128)(2,1)} slice(f32[2048,4096]{1,0:T(8,128)} %refs_0_.1), slice={[0:64], [0:4096]} | slice | bytes 1048576 | tf_op jit(solution)/shard_map/slice | solution.py:511
  19.0 2.9 %collective-permute-done.1 = f32[128,128]{1,0:T(8,128)S(1)} collective-permute-done((f32[128,128]{1,0:T(8,128)S(1)}, f32[128,128]{1,0:T(8,128)S(1)}, u32[]{:S(2)}, u32[]{:S(2)}) %collective-permute-start.1) | collective-permute-done | bytes 65568 | tf_op jit(solution)/shard_map/ppermute | solution.py:41
  22.4 1.6 %collective-permute-start.4 = (f32[4,96,128]{2,1,0:T(8,128)S(1)}, f32[4,96,128]{2,1,0:T(8,128)S(1)}, u32[]{:S(2)}, u32[]{:S(2)}) collective-permute-start(f32[4,96,128]{2,1,0:T(8,128)S(1)} %get-tuple-element.117), channel_id=1, source_target_pairs={{0,2},{1,3},{2,0},{3,1},{4,6},{5,7},{6,4},{7,5},{8,10},{9,11},{10,... | collective-permute-start | bytes 589832 | tf_op jit(solution)/shard_map/ppermute | solution.py:41
  24.0 1.5 %collective-permute-start.3 = (f32[4,96,128]{2,1,0:T(8,128)S(1)}, f32[4,96,128]{2,1,0:T(8,128)S(1)}, u32[]{:S(2)}, u32[]{:S(2)}) collective-permute-start(f32[4,96,128]{2,1,0:T(8,128)S(1)} %get-tuple-element.117), channel_id=1, source_target_pairs={{0,1},{1,0},{2,3},{3,2},{4,5},{5,4},{6,7},{7,6},{8,9},{9,8},{10,11... | collective-permute-start | bytes 589832 | tf_op jit(solution)/shard_map/ppermute | solution.py:41
  26.0 2.9 %fusion.1 = (f32[2048,32]{1,0:T(8,128)S(1)}, f32[2048,32]{1,0:T(8,128)S(1)}, f32[2048,32]{1,0:T(8,128)S(1)}, f32[2048,32]{1,0:T(8,128)S(1)}) fusion(f32[2048,4096]{1,0:T(8,128)} %refs_0_.1), kind=kLoop, calls=%fused_computation.23 | loop fusion | bytes 2097152 | tf_op jit(solution)/shard_map/slice | solution.py:504
  29.3 2.5 %collective-permute-done.3 = f32[4,96,128]{2,1,0:T(8,128)S(1)} collective-permute-done((f32[4,96,128]{2,1,0:T(8,128)S(1)}, f32[4,96,128]{2,1,0:T(8,128)S(1)}, u32[]{:S(2)}, u32[]{:S(2)}) %collective-permute-start.3) | collective-permute-done | bytes 196640 | tf_op jit(solution)/shard_map/ppermute | solution.py:41
  31.8 2.6 %collective-permute-done.5 = f32[4,96,128]{2,1,0:T(8,128)S(1)} collective-permute-done((f32[4,96,128]{2,1,0:T(8,128)S(1)}, f32[4,96,128]{2,1,0:T(8,128)S(1)}, u32[]{:S(2)}, u32[]{:S(2)}) %collective-permute-start.5) | collective-permute-done | bytes 196640 | tf_op jit(solution)/shard_map/ppermute | solution.py:41
  34.5 0.9 pad_maximum_fusion
  35.5 1.7 %collective-permute-start.12 = (f32[1024,128]{1,0:T(8,128)S(1)}, f32[1024,128]{1,0:T(8,128)}, u32[]{:S(2)}, u32[]{:S(2)}) collective-permute-start(f32[1024,128]{1,0:T(8,128)S(1)} %get-tuple-element.99.refs_12_), channel_id=1, source_target_pairs={{0,2},{1,3},{2,0},{3,1},{4,6},{5,7},{6,4},{7,5},{8,10},{9,11},{10,... | collective-permute-start | bytes 1572872 | tf_op jit(solution)/shard_map/ppermute | solution.py:41
  37.3 1.5 %collective-permute-start.10 = (f32[1024,128]{1,0:T(8,128)S(1)}, f32[1024,128]{1,0:T(8,128)}, u32[]{:S(2)}, u32[]{:S(2)}) collective-permute-start(f32[1024,128]{1,0:T(8,128)S(1)} %get-tuple-element.96.refs_8_), channel_id=1, source_target_pairs={{0,1},{1,0},{2,3},{3,2},{4,5},{5,4},{6,7},{7,6},{8,9},{9,8},{10,11... | collective-permute-start | bytes 1572872 | tf_op jit(solution)/shard_map/ppermute | solution.py:41
  39.4 0.6 pad_add_fusion.place
  40.8 0.9 copy-done.11
  41.6 9.2 %open_pivots.1 = (f32[256,256]{1,0:T(8,128)}, f32[256,256]{1,0:T(8,128)}, f32[256,128]{1,0:T(8,128)}, f32[8,256]{1,0:T(8,128)}, f32[256,512]{1,0:T(8,128)}, /*in...) custom-call(s32[2]{0:T(128)} %pad_add_fusion.place, f32[128]{0:T(128)} %convert_element_type.19.group_of, ...), custom_call_target="tpu_custom_call" | custom-call | flops 10000000000 | bytes 30000000 | tf_op jit(solution)/shard_map/open_pivots/pallas_call | solution.py:550
  51.8 3.6 %place_tiles.1 = (bf16[128,2048]{1,0:T(8,128)(2,1)}, bf16[128,2048]{1,0:T(8,128)(2,1)}, bf16[128,2048]{1,0:T(8,128)(2,1)}, bf16[128,2048]{1,0:T(8,128)(2,1)}) custom-call(s32[2]{0:T(128)} %pad_add_fusion.place, s32[128]{0:T(128)} %copy-done.9, bf16[8,64,2048]{2,1,0:T(8,128)(2,1)} %bitcast.20), custom_call_target="tpu_custom_call" | custom-call | bytes 65536 | tf_op jit(solution)/shard_map/place_tiles/pallas_call | solution.py:572
  55.5 1.6 %collective-permute-start.7 = (bf16[128,2048]{1,0:T(8,128)(2,1)}, bf16[128,2048]{1,0:T(8,128)(2,1)S(1)}, u32[]{:S(2)}, u32[]{:S(2)}) collective-permute-start(bf16[128,2048]{1,0:T(8,128)(2,1)} %get-tuple-element.74), channel_id=1, source_target_pairs={{0,1},{1,0},{2,3},{3,2},{4,5},{5,4},{6,7},{7,6},{8,9},{9,8},{10,11... | collective-permute-start | bytes 1572872 | tf_op jit(solution)/shard_map/ppermute | solution.py:41
  57.1 1.5 %collective-permute-start.8 = (bf16[128,2048]{1,0:T(8,128)(2,1)}, bf16[128,2048]{1,0:T(8,128)(2,1)S(1)}, u32[]{:S(2)}, u32[]{:S(2)}) collective-permute-start(bf16[128,2048]{1,0:T(8,128)(2,1)} %get-tuple-element.75), channel_id=1, source_target_pairs={{0,2},{1,3},{2,0},{3,1},{4,6},{5,7},{6,4},{7,5},{8,10},{9,11},{10,... | collective-permute-start | bytes 1572872 | tf_op jit(solution)/shard_map/ppermute | solution.py:41
  59.0 8.6 %first_pivots.1 = (f32[512,256]{1,0:T(8,128)}, bf16[256,256]{1,0:T(8,128)(2,1)}, bf16[256,256]{1,0:T(8,128)(2,1)}, bf16[256,256]{1,0:T(8,128)(2,1)}, bf16[256,25...) custom-call(f32[256,256]{1,0:T(8,128)} %get-tuple-element.65.begun, ...), custom_call_target="tpu_custom_call" | custom-call | flops 1000000000 | bytes 1000000 | tf_op jit(solution)/shard_map/first_pivots/pallas_call | solution.py:585
  67.6 13.7 %second_pivots.1 = (f32[256,256]{1,0:T(8,128)}, bf16[256,256]{1,0:T(8,128)(2,1)}, bf16[256,256]{1,0:T(8,128)(2,1)}, bf16[256,256]{1,0:T(8,128)(2,1)}, bf16[256,256]{1,0:T(8,128)(2,1)}) custom-call(f32[256,256]{1,0:T(8,128)} %get-tuple-element.71.rest), custom_call_target="tpu_custom_call" | custom-call | flops 2000000000 | bytes 1000000 | tf_op jit(solution)/shard_map/second_pivots/pallas_call | solution.py:598
  81.3 7.0 %collective-permute-done.9.refs_7_ = bf16[128,2048]{1,0:T(8,128)(2,1)S(1)} collective-permute-done((bf16[128,2048]{1,0:T(8,128)(2,1)}, bf16[128,2048]{1,0:T(8,128)(2,1)S(1)}, u32[]{:S(2)}, u32[]{:S(2)}) %collective-permute-start.9) | collective-permute-done | bytes 524320 | tf_op jit(solution)/shard_map/ppermute | solution.py:41
  88.4 0.7 copy-done.7
  89.4 0.8 copy-done.13
  91.2 0.8 collective-permute-done.14.far_kids.refs_3_
  92.1 1.0 copy-done.10
  93.0 9.1 %col_factors.1.refs_1_ = bf16[512,4096]{1,0:T(8,128)(2,1)} custom-call(s32[2]{0:T(128)} %pad_add_fusion.place, f32[128]{0:T(128)} %convert_element_type.19.group_of, f32[128]{0:T(128)} %compare_convert_fusion.kid_of, bf16[8,64,4096]{2,1,0:T(8,128)(2,1)} %bitcast.27, bf16[256,2048]{1,0:T(8,128)(2,1)} %copy-done, bf16[256,2048]{1,0:T(8,128)(2,1)} %copy-done.10, ...), custom_call_target="tpu_custom_call" | custom-call | flops 10000000000 | bytes 30000000 | tf_op jit(solution)/shard_map/col_factors/pallas_call | solution.py:617
  102.1 1.6 %collective-permute-done.15.refs_11_ = f32[1024,128]{1,0:T(8,128)S(1)} collective-permute-done((f32[1024,128]{1,0:T(8,128)S(1)}, f32[1024,128]{1,0:T(8,128)S(1)}, u32[]{:S(2)}, u32[]{:S(2)}) %collective-permute-start.15) | collective-permute-done | bytes 524320 | tf_op jit(solution)/shard_map/ppermute | solution.py:41
  104.5 29.9 %schur_update.1 = (f32[2048,4096]{1,0:T(8,128)}, bf16[2048,128]{1,0:T(8,128)(2,1)}) custom-call(s32[2]{0:T(128)} %pad_add_fusion.place, f32[128]{0:T(128)} %convert_element_type.19.group_of, f32[128]{0:T(128)} %compare_convert_fusion.kid_of, bf16[256,512]{1,0:T(8,128)(2,1)} %get-tuple-element.57.piv_t, f32[512,256]{1,0:T(8,128)} %get-tuple-element.70.lower1, ...), custom_call_target="tpu_custom_call" | custom-call | flops 30000001024 | bytes 90000000 | tf_op jit(solution)/shard_map/schur_update/pallas_call | solution.py:643
  (81 shorter events, 7.0 us)
Async XLA Ops:
  7.2 43.7 %all-gather.5.cloned.1.call-start = ((), (), s32[]{:S(2)}) async-start(), calls=%async_computation | async-start | bytes 2359296 | tf_op jit(solution)/shard_map/all_gather | solution.py:510
  7.9 84.2 %all-gather.7.cloned.1.call-start = ((), (), s32[]{:S(2)}) async-start(), calls=%async_computation.1 | async-start | bytes 4718592 | tf_op jit(solution)/shard_map/all_gather | solution.py:512
  11.1 7.9 %collective-permute-start.2 = (f32[128,128]{1,0:T(8,128)S(1)}, f32[128,128]{1,0:T(8,128)S(1)}, u32[]{:S(2)}, u32[]{:S(2)}) collective-permute-start(f32[128,128]{1,0:T(8,128)S(1)} %maximum_maximum_fusion), channel_id=1, source_target_pairs={{0,24},{4,28},{8,16},{12,20},{16,8},{20,12},{24,0},{28,4},{1,25},{... | collective-permute-start | bytes 196616 | tf_op jit(solution)/shard_map/ppermute | solution.py:41
  16.2 5.6 %collective-permute-start.1 = (f32[128,128]{1,0:T(8,128)S(1)}, f32[128,128]{1,0:T(8,128)S(1)}, u32[]{:S(2)}, u32[]{:S(2)}) collective-permute-start(f32[128,128]{1,0:T(8,128)S(1)} %maximum_maximum_fusion), channel_id=1, source_target_pairs={{0,16},{4,20},{8,24},{12,28},{16,0},{20,4},{24,8},{28,12},{1,17},{... | collective-permute-start | bytes 196616 | tf_op jit(solution)/shard_map/ppermute | solution.py:41
  16.2 5.6 %collective-permute-start = (f32[128,128]{1,0:T(8,128)S(1)}, f32[128,128]{1,0:T(8,128)S(1)}, u32[]{:S(2)}, u32[]{:S(2)}) collective-permute-start(f32[128,128]{1,0:T(8,128)S(1)} %maximum_maximum_fusion), channel_id=1, source_target_pairs={{0,8},{4,12},{8,0},{12,4},{16,24},{20,28},{24,16},{28,20},{1,9},{5... | collective-permute-start | bytes 196616 | tf_op jit(solution)/shard_map/ppermute | solution.py:41
  22.4 6.9 %collective-permute-start.4 = (f32[4,96,128]{2,1,0:T(8,128)S(1)}, f32[4,96,128]{2,1,0:T(8,128)S(1)}, u32[]{:S(2)}, u32[]{:S(2)}) collective-permute-start(f32[4,96,128]{2,1,0:T(8,128)S(1)} %get-tuple-element.117), channel_id=1, source_target_pairs={{0,2},{1,3},{2,0},{3,1},{4,6},{5,7},{6,4},{7,5},{8,10},{9,11},{10,... | collective-permute-start | bytes 589832 | tf_op jit(solution)/shard_map/ppermute | solution.py:41
  24.0 7.8 %collective-permute-start.3 = (f32[4,96,128]{2,1,0:T(8,128)S(1)}, f32[4,96,128]{2,1,0:T(8,128)S(1)}, u32[]{:S(2)}, u32[]{:S(2)}) collective-permute-start(f32[4,96,128]{2,1,0:T(8,128)S(1)} %get-tuple-element.117), channel_id=1, source_target_pairs={{0,1},{1,0},{2,3},{3,2},{4,5},{5,4},{6,7},{7,6},{8,9},{9,8},{10,11... | collective-permute-start | bytes 589832 | tf_op jit(solution)/shard_map/ppermute | solution.py:41
  25.5 8.9 %collective-permute-start.5 = (f32[4,96,128]{2,1,0:T(8,128)S(1)}, f32[4,96,128]{2,1,0:T(8,128)S(1)}, u32[]{:S(2)}, u32[]{:S(2)}) collective-permute-start(f32[4,96,128]{2,1,0:T(8,128)S(1)} %get-tuple-element.117), channel_id=1, source_target_pairs={{0,3},{1,2},{2,1},{3,0},{4,7},{5,6},{6,5},{7,4},{8,11},{9,10},{10,... | collective-permute-start | bytes 589832 | tf_op jit(solution)/shard_map/ppermute | solution.py:41
  34.4 1.0 copy-start.1
  34.4 6.3 %collective-permute-start.6 = (f32[4,4,96,128]{3,2,1,0:T(8,128)S(1)}, f32[4,4,96,128]{3,2,1,0:T(8,128)S(1)}, u32[]{:S(2)}, u32[]{:S(2)}) collective-permute-start(f32[4,4,96,128]{3,2,1,0:T(8,128)S(1)} %pad_maximum_fusion.2.near), channel_id=1, source_target_pairs={{0,4},{4,0},{8,12},{12,8},{16,20},{20,16},{24,28},{28,24},{1,5},{5... | collective-permute-start | bytes 2359304 | tf_op jit(solution)/shard_map/ppermute | solution.py:41
  35.4 3.3 %copy-start.15 = (s32[32]{0:T(128)S(1)}, s32[32]{0:T(128)}, u32[]{:S(2)}) copy-start(s32[32]{0:T(128)} %param.5) | copy-start | bytes 388
  35.4 4.7 %copy-start.8 = (s32[128]{0:T(128)S(1)}, s32[128]{0:T(128)}, u32[]{:S(2)}) copy-start(s32[128]{0:T(128)} %param.7) | copy-start | bytes 1540
  35.5 15.3 %copy-start.3 = (f32[1024,128]{1,0:T(8,128)}, f32[1024,128]{1,0:T(8,128)S(1)}, u32[]{:S(2)}) copy-start(f32[1024,128]{1,0:T(8,128)S(1)} %get-tuple-element.96.refs_8_) | copy-start | bytes 1572868
  35.5 15.9 %copy-start.2 = (f32[1024,128]{1,0:T(8,128)}, f32[1024,128]{1,0:T(8,128)S(1)}, u32[]{:S(2)}) copy-start(f32[1024,128]{1,0:T(8,128)S(1)} %get-tuple-element.99.refs_12_) | copy-start | bytes 1572868
  35.5 21.6 %collective-permute-start.12 = (f32[1024,128]{1,0:T(8,128)S(1)}, f32[1024,128]{1,0:T(8,128)}, u32[]{:S(2)}, u32[]{:S(2)}) collective-permute-start(f32[1024,128]{1,0:T(8,128)S(1)} %get-tuple-element.99.refs_12_), channel_id=1, source_target_pairs={{0,2},{1,3},{2,0},{3,1},{4,6},{5,7},{6,4},{7,5},{8,10},{9,11},{10,... | collective-permute-start | bytes 1572872 | tf_op jit(solution)/shard_map/ppermute | solution.py:41
  37.3 21.3 %collective-permute-start.10 = (f32[1024,128]{1,0:T(8,128)S(1)}, f32[1024,128]{1,0:T(8,128)}, u32[]{:S(2)}, u32[]{:S(2)}) collective-permute-start(f32[1024,128]{1,0:T(8,128)S(1)} %get-tuple-element.96.refs_8_), channel_id=1, source_target_pairs={{0,1},{1,0},{2,3},{3,2},{4,5},{5,4},{6,7},{7,6},{8,9},{9,8},{10,11... | collective-permute-start | bytes 1572872 | tf_op jit(solution)/shard_map/ppermute | solution.py:41
  40.2 10.7 %copy-start.9 = (s32[128]{0:T(128)}, s32[128]{0:T(128)S(1)}, u32[]{:S(2)}) copy-start(s32[128]{0:T(128)S(1)} %select_reduce_fusion.inverse_map) | copy-start | bytes 1540
  50.9 30.4 %collective-permute-start.11 = (f32[1024,128]{1,0:T(8,128)S(1)}, f32[1024,128]{1,0:T(8,128)S(1)}, u32[]{:S(2)}, u32[]{:S(2)}) collective-permute-start(f32[1024,128]{1,0:T(8,128)S(1)} %get-tuple-element.96.refs_8_), channel_id=1, source_target_pairs={{0,2},{1,3},{2,0},{3,1},{4,6},{5,7},{6,4},{7,5},{8,10},{9,11},{10,... | collective-permute-start | bytes 1572872 | tf_op jit(solution)/shard_map/ppermute | solution.py:41
  51.4 29.9 %collective-permute-start.13 = (f32[1024,128]{1,0:T(8,128)S(1)}, f32[1024,128]{1,0:T(8,128)}, u32[]{:S(2)}, u32[]{:S(2)}) collective-permute-start(f32[1024,128]{1,0:T(8,128)S(1)} %get-tuple-element.99.refs_12_), channel_id=1, source_target_pairs={{0,1},{1,0},{2,3},{3,2},{4,5},{5,4},{6,7},{7,6},{8,9},{9,8},{10,11... | collective-permute-start | bytes 1572872 | tf_op jit(solution)/shard_map/ppermute | solution.py:41
  55.5 25.8 %collective-permute-start.7 = (bf16[128,2048]{1,0:T(8,128)(2,1)}, bf16[128,2048]{1,0:T(8,128)(2,1)S(1)}, u32[]{:S(2)}, u32[]{:S(2)}) collective-permute-start(bf16[128,2048]{1,0:T(8,128)(2,1)} %get-tuple-element.74), channel_id=1, source_target_pairs={{0,1},{1,0},{2,3},{3,2},{4,5},{5,4},{6,7},{7,6},{8,9},{9,8},{10,11... | collective-permute-start | bytes 1572872 | tf_op jit(solution)/shard_map/ppermute | solution.py:41
  57.1 24.2 %collective-permute-start.8 = (bf16[128,2048]{1,0:T(8,128)(2,1)}, bf16[128,2048]{1,0:T(8,128)(2,1)S(1)}, u32[]{:S(2)}, u32[]{:S(2)}) collective-permute-start(bf16[128,2048]{1,0:T(8,128)(2,1)} %get-tuple-element.75), channel_id=1, source_target_pairs={{0,2},{1,3},{2,0},{3,1},{4,6},{5,7},{6,4},{7,5},{8,10},{9,11},{10,... | collective-permute-start | bytes 1572872 | tf_op jit(solution)/shard_map/ppermute | solution.py:41
  58.6 29.7 %collective-permute-start.9 = (bf16[128,2048]{1,0:T(8,128)(2,1)}, bf16[128,2048]{1,0:T(8,128)(2,1)S(1)}, u32[]{:S(2)}, u32[]{:S(2)}) collective-permute-start(bf16[128,2048]{1,0:T(8,128)(2,1)} %get-tuple-element.76), channel_id=1, source_target_pairs={{0,3},{1,2},{2,1},{3,0},{4,7},{5,6},{6,5},{7,4},{8,11},{9,10},{10,... | collective-permute-start | bytes 1572872 | tf_op jit(solution)/shard_map/ppermute | solution.py:41
  67.6 20.8 %copy-start.4 = (bf16[128,2048]{1,0:T(8,128)(2,1)S(1)}, bf16[128,2048]{1,0:T(8,128)(2,1)}, u32[]{:S(2)}) copy-start(bf16[128,2048]{1,0:T(8,128)(2,1)} %get-tuple-element.86.refs_4_) | copy-start | bytes 1572868
  81.3 7.1 %copy-start.12 = (f32[1024,128]{1,0:T(8,128)}, f32[1024,128]{1,0:T(8,128)S(1)}, u32[]{:S(2)}) copy-start(f32[1024,128]{1,0:T(8,128)S(1)} %collective-permute-done.11.refs_10_) | copy-start | bytes 1572868
  81.3 8.0 %copy-start.5 = (bf16[128,2048]{1,0:T(8,128)(2,1)}, bf16[128,2048]{1,0:T(8,128)(2,1)S(1)}, u32[]{:S(2)}) copy-start(bf16[128,2048]{1,0:T(8,128)(2,1)S(1)} %collective-permute-done.7.refs_5_) | copy-start | bytes 1572868
  81.3 8.0 %copy-start.6 = (bf16[128,2048]{1,0:T(8,128)(2,1)}, bf16[128,2048]{1,0:T(8,128)(2,1)S(1)}, u32[]{:S(2)}) copy-start(bf16[128,2048]{1,0:T(8,128)(2,1)S(1)} %collective-permute-done.8.refs_6_) | copy-start | bytes 1572868
  89.2 1.0 copy-start.13
  89.3 2.7 %copy-start = (bf16[256,2048]{1,0:T(8,128)(2,1)}, bf16[256,2048]{1,0:T(8,128)(2,1)S(1)}, u32[]{:S(2)}) copy-start(bf16[256,2048]{1,0:T(8,128)(2,1)S(1)} %pad_maximum_fusion.1.near_kids.refs_2_) | copy-start | bytes 3145732
  89.3 2.7 %collective-permute-start.14 = (bf16[256,2048]{1,0:T(8,128)(2,1)S(1)}, bf16[256,2048]{1,0:T(8,128)(2,1)S(1)}, u32[]{:S(2)}, u32[]{:S(2)}) collective-permute-start(bf16[256,2048]{1,0:T(8,128)(2,1)S(1)} %pad_maximum_fusion.1.near_kids.refs_2_), channel_id=1, source_target_pairs={{0,4},{4,0},{8,12},{12,8},{16,20},{20,16},{24,28},{28,24},{1,5},{5... | collective-permute-start | bytes 3145736 | tf_op jit(solution)/shard_map/ppermute | solution.py:41
  90.2 13.5 %collective-permute-start.15 = (f32[1024,128]{1,0:T(8,128)S(1)}, f32[1024,128]{1,0:T(8,128)S(1)}, u32[]{:S(2)}, u32[]{:S(2)}) collective-permute-start(f32[1024,128]{1,0:T(8,128)S(1)} %copy-done.13), channel_id=1, source_target_pairs={{0,1},{1,0},{2,3},{3,2},{4,5},{5,4},{6,7},{7,6},{8,9},{9,8},{10,11... | collective-permute-start | bytes 1572872 | tf_op jit(solution)/shard_map/ppermute | solution.py:41
  90.7 13.5 %collective-permute-start.16 = (f32[1024,128]{1,0:T(8,128)}, f32[1024,128]{1,0:T(8,128)}, u32[]{:S(2)}, u32[]{:S(2)}) collective-permute-start(f32[1024,128]{1,0:T(8,128)} %collective-permute-done.13.refs_14_), channel_id=1, source_target_pairs={{0,2},{1,3},{2,0},{3,1},{4,6},{5,7},{6,4},{7,5},{8,10},{9,11},{10,... | collective-permute-start | bytes 1572872 | tf_op jit(solution)/shard_map/ppermute | solution.py:41
  92.0 1.0 copy-start.10
  (3 other events, 2.5 us)
Sparse Core Ops, SparseCore 0:
  9.6 31.7 all-gather.4
  43.0 46.8 all-gather.6
